TPU v7x, 32 devices: a whole 2x2x4 slice. The times are simulated.
32 devices in a mesh: mem: 4 (over z), pipe: 4 (over y, x), dp: 2 (over core).
Axes of the slice: x: 2, y: 2, z: 4, core: 2. Of those that a mesh axis runs over, the one named last changes fastest.
Arguments:
- values: bfloat16 [4096, 4096], P(('dp', 'mem'), 'pipe'), parts along dimension 0, may hold values from -6 to 6
- cotangent: bfloat16 [1024, 4096], P(('dp', 'mem'), 'pipe'), parts along dimension 0, may hold values from -6 to 6
- scores: float32 [1024, 4, 32], P(('dp', 'mem')), parts along dimension 0, may hold values from -8 to 410, as said below
- row_lists: int32 [8, 4, 128], P(('dp', 'mem')), parts along dimension 0, may hold values from -1 to 511, as said below
- sel_slot: int32 [1024, 4, 32], P(('dp', 'mem')), parts along dimension 0, may hold values from 0 to 511, as said below
Outputs:
- mem_out: bfloat16 [1024, 4096], P(('dp', 'mem'), 'pipe'), parts along dimension 0
- grad_values: bfloat16 [4096, 4096], P(('dp', 'mem'), 'pipe'), parts along dimension 0
- grad_scores: float32 [1024, 4, 32], P(('dp', 'mem')), parts along dimension 0
There are 2 independent parts, one for each index of `dp`. A program takes and returns all parts, laid end to end along the dimension named above; each array names one. Nothing has to cross between parts.
Inputs may be any that keep to these rules, and one draw needn't show every extreme that they name: `row_lists`: each entry is a row of the owner's shard, or -1 for an empty slot; the rows of one block are distinct and its empty slots come last; in every draw some owner receives full blocks of 128 rows from every device. `sel_slot`: each entry names a slot of the request blocks of the token's own mem index, and that slot holds a row; the 32 entries of one token and head are distinct. `scores`: scores are finite.
All inputs are finite; a program needn't handle non-finite values.
Results may differ from a plain program's by a relative error of at most 0.013.
Values may be sent and summed in bfloat16 or wider, within the bound.
A program may use at most 128 MiB of HBM per device.

v0:
```python
import jax
import jax.numpy as jnp
from jax import lax
from jax.sharding import PartitionSpec as P


def shards(values, cotangent, scores, row_lists, sel_slot):
    owners = lax.axis_size("mem")
    tokens_here = cotangent.shape[0]
    cap_slots = row_lists.shape[2]
    slot_count = owners * cap_slots
    width = values.shape[1]
    table_rows = values.shape[0]
    highest = lax.Precision.HIGHEST
    weights = jax.nn.softmax(scores, axis=-1)
    chosen = sel_slot.reshape(tokens_here, -1)
    owner_of = chosen // cap_slots
    place_of = chosen % cap_slots
    owner_hot = (owner_of[..., None] == jnp.arange(owners, dtype=jnp.int32)[None, None, :]).astype(
        jnp.float32
    )
    place_hot = (
        place_of[..., None] == jnp.arange(cap_slots, dtype=jnp.int32)[None, None, :]
    ).astype(jnp.float32)
    weighted_owner = owner_hot * weights.reshape(tokens_here, -1)[..., None]
    combined = jnp.einsum(
        "tpo,tpc->toc",
        weighted_owner,
        place_hot,
        precision=highest,
        preferred_element_type=jnp.float32,
    )
    combined = combined.reshape(tokens_here, slot_count).astype(jnp.bfloat16)
    asked = lax.all_to_all(row_lists[0], "mem", split_axis=0, concat_axis=0, tiled=True)
    present = asked >= 0
    looked = jnp.take(values, jnp.maximum(asked, 0), axis=0)
    looked = jnp.where(present[..., None], looked, jnp.zeros_like(looked))
    replied = lax.all_to_all(looked, "mem", split_axis=0, concat_axis=0, tiled=True)
    gathered_rows = replied.reshape(slot_count, width)
    mem_out = jnp.dot(combined, gathered_rows, preferred_element_type=jnp.float32).astype(
        jnp.bfloat16
    )
    products = lax.dot_general(
        cotangent, gathered_rows, (((1,), (1,)), ((), ())), preferred_element_type=jnp.float32
    )
    products = products.reshape(tokens_here, owners, cap_slots)
    picked = jnp.einsum(
        "tpc,toc->tpo", place_hot, products, precision=highest, preferred_element_type=jnp.float32
    )
    partial_dots = jnp.sum(picked * owner_hot, axis=-1).reshape(weights.shape)
    full_dots = lax.psum(partial_dots.astype(jnp.bfloat16), "pipe").astype(jnp.float32)
    grad_scores = weights * (full_dots - jnp.sum(weights * full_dots, axis=-1, keepdims=True))
    sums_here = lax.dot_general(
        combined, cotangent, (((0,), (0,)), ((), ())), preferred_element_type=jnp.float32
    )
    received = lax.all_to_all(
        sums_here.reshape(owners, cap_slots, width).astype(jnp.bfloat16),
        "mem",
        split_axis=0,
        concat_axis=0,
        tiled=True,
    ).astype(jnp.float32)
    received = received.reshape(-1, width)
    upper_part = received.astype(jnp.bfloat16)
    lower_part = (received - upper_part.astype(jnp.float32)).astype(jnp.bfloat16)
    row_hot = (
        asked.reshape(-1)[:, None] == jnp.arange(table_rows, dtype=jnp.int32)[None, :]
    ).astype(jnp.bfloat16)
    contract = (((0,), (0,)), ((), ()))
    grad_full = lax.dot_general(row_hot, upper_part, contract, preferred_element_type=jnp.float32)
    grad_full = grad_full + lax.dot_general(
        row_hot, lower_part, contract, preferred_element_type=jnp.float32
    )
    grad_values = grad_full.astype(jnp.bfloat16)
    return (mem_out, grad_values, grad_scores)


def solution(mesh):
    placed = (
        P(("dp", "mem"), "pipe"),
        P(("dp", "mem"), "pipe"),
        P(("dp", "mem"), None, None),
        P(("dp", "mem"), None, None),
        P(("dp", "mem"), None, None),
    )
    return jax.shard_map(
        shards,
        mesh=mesh,
        in_specs=placed,
        out_specs=(
            P(("dp", "mem"), "pipe"),
            P(("dp", "mem"), "pipe"),
            P(("dp", "mem"), None, None),
        ),
        check_vma=False,
    )
```

profile of v0, /device:TPU:0, one launch (start us, length us, event | category | flops | bytes accessed | tf_op | source)
XLA Modules:
  0.0 103.0 jit_solution(237981833054110883)
XLA Ops:
  0.6 0.0 copy-start
  0.6 0.0 copy-start.1
  0.7 6.5 %all-to-all-start = ((s32[4,1,128]{2,1,0:T(1,128)}), s32[4,1,128]{2,1,0:T(1,128)S(1)}, u32[]{:S(2)}, u32[]{:S(2)}) async-start(s32[4,1,128]{2,1,0:T(1,128)} %bitcast.52), calls=%async_computation | async-start | bytes 4096 | tf_op jit(solution)/shard_map/all_to_all | solution.py:34
  7.1 1.0 fusion.12
  8.1 0.0 copy-start.2
  8.1 0.1 copy.29
  8.2 0.5 copy-done.2
  8.7 0.9 copy.25
  9.6 0.1 add_select_fusion.1
  9.7 0.0 copy-start.4
  9.7 0.0 copy-start.6
  9.7 5.8 %fusion.9 = bf16[128,4,128]{2,1,0:T(4,128)(2,1)S(1)} fusion(s32[128,128]{1,0:T(8,128)S(1)} %get-tuple-element.4, f32[128,128]{1,0:T(8,128)S(1)} %copy.29, s32[128,128]{1,0:T(8,128)S(1)} %get-tuple-element.3), kind=kOutput, calls=%fused_computation.15 | convolution fusion | flops 102957056 | bytes 327680 | tf_op jit(solution)/shard_map/tpo,tpc->toc/dot_general | solution.py:26
  15.6 0.0 copy-done.4
  15.6 0.0 copy-done.6
  15.6 0.1 copy.31
  15.7 0.0 copy-done.1
  15.8 1.4 %convolution_convert_fusion = bf16[4,128,1024]{2,1,0:T(8,128)(2,1)} fusion(bf16[4,128,128]{2,1,0:T(8,128)(2,1)S(1)} %bitcast.45, bf16[128,1024]{1,0:T(8,128)(2,1)S(1)} %copy-done.1), kind=kOutput, calls=%fused_computation.11 | convolution fusion | flops 134742016 | bytes 1441792 | tf_op jit(solution)/shard_map/dot_general | solution.py:53
  17.1 0.0 all-to-all-done
  17.1 5.1 %all-to-all-start.2 = ((bf16[4,128,1024]{2,1,0:T(8,128)(2,1)}), bf16[4,128,1024]{2,1,0:T(8,128)(2,1)S(1)}, u32[]{:S(2)}, u32[]{:S(2)}) async-start(bf16[4,128,1024]{2,1,0:T(8,128)(2,1)} %convolution_convert_fusion), calls=%async_computation.2 | async-start | bytes 2097152 | tf_op jit(solution)/shard_map/all_to_all | solution.py:56
  22.3 0.0 copy-done
  22.3 2.1 %gather_fusion = bf16[512,1024]{1,0:T(8,128)(2,1)S(1)} fusion(bf16[512,1024]{1,0:T(8,128)(2,1)S(1)} %copy-done, s32[1024]{0:T(1024)S(1)} %pad_clamp_fusion), kind=kCustom, calls=%fused_computation | custom fusion | bytes 2099200 | tf_op jit(solution)/shard_map/jit(_take)/gather | solution.py:36
  24.4 1.2 %select_select_fusion = bf16[4,128,1024]{2,1,0:T(8,128)(2,1)} fusion(bf16[4,128,1024]{2,1,0:T(8,128)(2,1)S(1)} %bitcast.39, pred[4,128]{1,0:T(4,128)(4,1)S(1)} %get-tuple-element.7, pred[4,128]{1,0:T(4,128)(4,1)S(1)} %get-tuple-element.8), kind=kLoop, calls=%fused_computation.24 | loop fusion | flops 1048576 | bytes 2098176 | tf_op jit(solution)/shard_map/jit(_where)/select_n | solution.py:37
  25.6 21.8 %all-to-all-done.2 = bf16[4,128,1024]{2,1,0:T(8,128)(2,1)S(1)} async-done(((bf16[4,128,1024]{2,1,0:T(8,128)(2,1)}), bf16[4,128,1024]{2,1,0:T(8,128)(2,1)S(1)}, u32[]{:S(2)}, u32[]{:S(2)}) %all-to-all-start.2) | async-done | bytes 1048608 | tf_op jit(solution)/shard_map/all_to_all | solution.py:56
  47.4 3.5 %all-to-all-start.1 = ((bf16[4,128,1024]{2,1,0:T(8,128)(2,1)}), bf16[4,128,1024]{2,1,0:T(8,128)(2,1)S(1)}, u32[]{:S(2)}, u32[]{:S(2)}) async-start(bf16[4,128,1024]{2,1,0:T(8,128)(2,1)} %select_select_fusion), calls=%async_computation.1 | async-start | bytes 2097152 | tf_op jit(solution)/shard_map/all_to_all | solution.py:38
  50.9 0.8 fusion.16
  51.8 1.8 %add_convert_fusion = bf16[512,1024]{1,0:T(8,128)(2,1)} fusion(f32[512,1024]{1,0:T(8,128)S(1)} %fusion.16, bf16[512,1024]{1,0:T(8,128)(2,1)S(1)} %bitcast.41, s32[512]{0:T(512)S(1)} %bitcast.50), kind=kOutput, calls=%fused_computation.9 | convolution fusion | flops 539754496 | bytes 4196352 | tf_op jit(solution)/shard_map/dot_general | solution.py:71
  53.6 0.0 copy-start.5
  53.6 0.0 copy-start.7
  53.6 22.5 %all-to-all-done.1 = bf16[4,128,1024]{2,1,0:T(8,128)(2,1)S(1)} async-done(((bf16[4,128,1024]{2,1,0:T(8,128)(2,1)}), bf16[4,128,1024]{2,1,0:T(8,128)(2,1)S(1)}, u32[]{:S(2)}, u32[]{:S(2)}) %all-to-all-start.1) | async-done | bytes 1048608 | tf_op jit(solution)/shard_map/all_to_all | solution.py:38
  76.1 0.4 fusion.30
  76.6 0.1 copy.32
  76.7 0.0 copy-done.5
  76.7 0.0 copy-done.7
  76.7 0.0 copy-start.3
  76.7 8.1 %fusion.10 = bf16[128,128]{1,0:T(8,128)(2,1)S(1)} fusion(f32[128,4,128]{2,1,0:T(4,128)S(1)} %copy.32, s32[128,128]{1,0:T(8,128)S(1)} %copy-done.7, s32[128,128]{1,0:T(8,128)S(1)} %copy-done.5), kind=kOutput, calls=%fused_computation.16 | convolution fusion | flops 102940672 | bytes 425984 | tf_op jit(solution)/shard_map/tpc,toc->tpo/dot_general | solution.py:47
  84.9 0.1 copy.33
  85.0 16.3 %psum.7 = bf16[128,4,32]{0,2,1:T(8,128)(2,1)S(1)} all-reduce(bf16[128,4,32]{0,2,1:T(8,128)(2,1)S(1)} %bitcast.47), channel_id=1, replica_groups=mesh['mem'=4,'pipe'=4,'dp'=2] {'pipe'}, use_global_device_ids=true, to_apply=%region_3.4 | all-reduce | flops 16384 | bytes 65536 | tf_op jit(solution)/shard_map/psum | solution.py:51
  101.3 0.0 copy-done.3
  101.3 0.7 fusion.15
  101.9 1.0 fusion.7
  (5 shorter events, 0.1 us)
Async XLA Ops:
  0.6 21.6 %copy-start = (bf16[512,1024]{1,0:T(8,128)(2,1)S(1)}, bf16[512,1024]{1,0:T(8,128)(2,1)}, u32[]{:S(2)}) copy-start(bf16[512,1024]{1,0:T(8,128)(2,1)} %param.5) | copy-start | bytes 3145732
  0.6 15.1 %copy-start.1 = (bf16[128,1024]{1,0:T(8,128)(2,1)S(1)}, bf16[128,1024]{1,0:T(8,128)(2,1)}, u32[]{:S(2)}) copy-start(bf16[128,1024]{1,0:T(8,128)(2,1)} %param.6) | copy-start | bytes 786436
  0.7 16.5 %all-to-all-start = ((s32[4,1,128]{2,1,0:T(1,128)}), s32[4,1,128]{2,1,0:T(1,128)S(1)}, u32[]{:S(2)}, u32[]{:S(2)}) async-start(s32[4,1,128]{2,1,0:T(1,128)} %bitcast.52), calls=%async_computation | async-start | bytes 4096 | tf_op jit(solution)/shard_map/all_to_all | solution.py:34
  8.1 0.6 copy-start.2
  9.7 5.9 %copy-start.4 = (s32[128,128]{1,0:T(8,128)}, s32[128,128]{1,0:T(8,128)S(1)}, u32[]{:S(2)}) copy-start(s32[128,128]{1,0:T(8,128)S(1)} %get-tuple-element.3) | copy-start | bytes 196612
  9.7 5.9 %copy-start.6 = (s32[128,128]{1,0:T(8,128)}, s32[128,128]{1,0:T(8,128)S(1)}, u32[]{:S(2)}) copy-start(s32[128,128]{1,0:T(8,128)S(1)} %get-tuple-element.4) | copy-start | bytes 196612
  17.1 30.3 %all-to-all-start.2 = ((bf16[4,128,1024]{2,1,0:T(8,128)(2,1)}), bf16[4,128,1024]{2,1,0:T(8,128)(2,1)S(1)}, u32[]{:S(2)}, u32[]{:S(2)}) async-start(bf16[4,128,1024]{2,1,0:T(8,128)(2,1)} %convolution_convert_fusion), calls=%async_computation.2 | async-start | bytes 2097152 | tf_op jit(solution)/shard_map/all_to_all | solution.py:56
  47.4 28.7 %all-to-all-start.1 = ((bf16[4,128,1024]{2,1,0:T(8,128)(2,1)}), bf16[4,128,1024]{2,1,0:T(8,128)(2,1)S(1)}, u32[]{:S(2)}, u32[]{:S(2)}) async-start(bf16[4,128,1024]{2,1,0:T(8,128)(2,1)} %select_select_fusion), calls=%async_computation.1 | async-start | bytes 2097152 | tf_op jit(solution)/shard_map/all_to_all | solution.py:38
  53.6 23.1 %copy-start.5 = (s32[128,128]{1,0:T(8,128)S(1)}, s32[128,128]{1,0:T(8,128)}, u32[]{:S(2)}) copy-start(s32[128,128]{1,0:T(8,128)} %copy-done.4) | copy-start | bytes 196612
  53.6 23.2 %copy-start.7 = (s32[128,128]{1,0:T(8,128)S(1)}, s32[128,128]{1,0:T(8,128)}, u32[]{:S(2)}) copy-start(s32[128,128]{1,0:T(8,128)} %copy-done.6) | copy-start | bytes 196612
  76.7 24.6 %copy-start.3 = (f32[128,4,32]{0,2,1:T(8,128)S(1)}, f32[128,4,32]{0,2,1:T(8,128)}, u32[]{:S(2)}) copy-start(f32[128,4,32]{0,2,1:T(8,128)} %copy-done.2) | copy-start | bytes 196612
where the time goes:
time: 103 us
  waiting for transfers between devices  44.4 us (43%)
  matrix products  19.4 us (19%)
  blocking collectives  16.3 us (16%)
  starting transfers between devices  15.1 us (15%)
  local copies, waits for them, and re-layouts  4.05 us (4%)
  other arithmetic  2.89 us (3%)
    all_to_all x1, waiting for transfers between devices, shards(): lax.all_to_all(looked, 'mem', split_axis=0, concat_axis=0, tiled=True)  22.5 us
    all_to_all x1, waiting for transfers between devices, shards(): lax.all_to_all(sums_here.reshape(owners, cap_slots, width).astype(jnp.bfl...  21.8 us
    psum x1, blocking collectives, shards(): lax.psum(partial_dots.astype(jnp.bfloat16), 'pipe').astype(jnp.float32)  16.3 us
    dot_general x1, matrix products, shards(): jnp.einsum('tpc,toc->tpo', place_hot, products, precision=highest, prefer...  8.1 us
    all_to_all x1, starting transfers between devices, shards(): lax.all_to_all(row_lists[0], 'mem', split_axis=0, concat_axis=0, tiled=True)  6.46 us
    dot_general x1, matrix products, shards(): jnp.einsum('tpo,tpc->toc', weighted_owner, place_hot, precision=highest,...  5.83 us
    all_to_all x1, starting transfers between devices, shards(): lax.all_to_all(sums_here.reshape(owners, cap_slots, width).astype(jnp.bfl...  5.09 us
    all_to_all x1, starting transfers between devices, shards(): lax.all_to_all(looked, 'mem', split_axis=0, concat_axis=0, tiled=True)  3.52 us
  transfers between devices with their start and end apart: 3, of which 2 were waited for; matrix products, arithmetic and copies ran while one was open for 15% of the time, Pallas kernels for 0%

commit v1 on v0

--- a/solution.py
+++ b/solution.py
@@ -1,10 +1,14 @@
+import functools
+
 import jax
 import jax.numpy as jnp
 from jax import lax
+from jax.experimental import pallas as pl
+from jax.experimental.pallas import tpu as pltpu
 from jax.sharding import PartitionSpec as P
 
 
-def shards(values, cotangent, scores, row_lists, sel_slot):
+def shards_collective(values, cotangent, scores, row_lists, sel_slot):
     owners = lax.axis_size("mem")
     tokens_here = cotangent.shape[0]
     cap_slots = row_lists.shape[2]
@@ -75,7 +79,459 @@
     return (mem_out, grad_values, grad_scores)
 
 
+MESH = pl.DeviceIdType.MESH
+CHUNKS = 4
+F32 = jnp.float32
+BF16 = jnp.bfloat16
+
+
+def kernel(
+    n,
+    pipes,
+    heads,
+    topk,
+    values_ref,
+    cot_ref,
+    scores_ref,
+    rows_ref,
+    sel_ref,
+    mem_ref,
+    grad_ref,
+    dscore_ref,
+    cot_all,
+    weights,
+    comb_own,
+    comb_in,
+    rows_in,
+    hot,
+    spread,
+    part,
+    from_left,
+    from_right,
+    prod_out,
+    prod_in,
+    dots_in,
+    ag_send,
+    ag_recv,
+    cb_send,
+    cb_recv,
+    rl_send,
+    rl_recv,
+    rs_send,
+    rs_recv,
+    pr_send,
+    pr_recv,
+    dt_send,
+    dt_recv,
+):
+    me = lax.axis_index("mem")
+    my_pipe = lax.axis_index("pipe")
+    tokens, width = cot_ref.shape
+    table_rows = values_ref.shape[0]
+    cap = rows_ref.shape[2]
+    step = tokens // CHUNKS
+    picks = heads * topk
+
+    def peer(d):
+        return lax.rem(me + d, n)
+
+    def pipe_peer(d):
+        return lax.rem(my_pipe + d, pipes)
+
+    barrier = pltpu.get_barrier_semaphore()
+    for d in range(1, n):
+        pl.semaphore_signal(barrier, inc=1, device_id={"mem": peer(d)}, device_id_type=MESH)
+    for d in range(1, pipes):
+        pl.semaphore_signal(
+            barrier, inc=1, device_id={"pipe": pipe_peer(d)}, device_id_type=MESH
+        )
+    pl.semaphore_wait(barrier, n - 1 + pipes - 1)
+
+    def rows_of(c):
+        return pl.ds(c * step, step)
+
+    def gather_copy(side, source, c, own=False):
+        to = me + 1 if side == 0 else me - 1
+        src = cot_ref.at[rows_of(c)] if own else cot_all.at[source, rows_of(c)]
+        return pltpu.make_async_remote_copy(
+            src_ref=src,
+            dst_ref=cot_all.at[source, rows_of(c)],
+            send_sem=ag_send.at[side, source, c],
+            recv_sem=ag_recv.at[source, c],
+            device_id={"mem": to},
+            device_id_type=MESH,
+        )
+
+    def sum_copy(side, dest, c):
+        to = me + 1 if side == 0 else me - 1
+        buf = from_left if side == 0 else from_right
+        return pltpu.make_async_remote_copy(
+            src_ref=buf.at[dest, rows_of(c)],
+            dst_ref=buf.at[dest, rows_of(c)],
+            send_sem=rs_send.at[side, dest, c],
+            recv_sem=rs_recv.at[side, dest, c],
+            device_id={"mem": to},
+            device_id_type=MESH,
+        )
+
+    def list_copy(to):
+        return pltpu.make_async_remote_copy(
+            src_ref=rows_ref.at[to],
+            dst_ref=rows_in.at[me],
+            send_sem=rl_send.at[to],
+            recv_sem=rl_recv.at[me],
+            device_id={"mem": to},
+            device_id_type=MESH,
+        )
+
+    def list_arrival(source):
+        return pltpu.make_async_remote_copy(
+            src_ref=rows_in.at[source],
+            dst_ref=rows_in.at[source],
+            send_sem=rl_send.at[source],
+            recv_sem=rl_recv.at[source],
+            device_id={"mem": source},
+            device_id_type=MESH,
+        )
+
+    def comb_copy(to):
+        return pltpu.make_async_remote_copy(
+            src_ref=comb_own.at[to],
+            dst_ref=comb_in.at[me],
+            send_sem=cb_send.at[to],
+            recv_sem=cb_recv.at[me],
+            device_id={"mem": to},
+            device_id_type=MESH,
+        )
+
+    def comb_arrival(source):
+        return pltpu.make_async_remote_copy(
+            src_ref=comb_in.at[source],
+            dst_ref=comb_in.at[source],
+            send_sem=cb_send.at[source],
+            recv_sem=cb_recv.at[source],
+            device_id={"mem": source},
+            device_id_type=MESH,
+        )
+
+    def prod_copy(to):
+        return pltpu.make_async_remote_copy(
+            src_ref=prod_out.at[to],
+            dst_ref=prod_in.at[me],
+            send_sem=pr_send.at[to],
+            recv_sem=pr_recv.at[me],
+            device_id={"mem": to},
+            device_id_type=MESH,
+        )
+
+    def prod_arrival(source):
+        return pltpu.make_async_remote_copy(
+            src_ref=prod_in.at[source],
+            dst_ref=prod_in.at[source],
+            send_sem=pr_send.at[source],
+            recv_sem=pr_recv.at[source],
+            device_id={"mem": source},
+            device_id_type=MESH,
+        )
+
+    def dots_copy(to):
+        return pltpu.make_async_remote_copy(
+            src_ref=dots_in.at[my_pipe],
+            dst_ref=dots_in.at[my_pipe],
+            send_sem=dt_send.at[to],
+            recv_sem=dt_recv.at[my_pipe],
+            device_id={"pipe": to},
+            device_id_type=MESH,
+        )
+
+    def dots_arrival(source):
+        return pltpu.make_async_remote_copy(
+            src_ref=dots_in.at[source],
+            dst_ref=dots_in.at[source],
+            send_sem=dt_send.at[source],
+            recv_sem=dt_recv.at[source],
+            device_id={"pipe": source},
+            device_id_type=MESH,
+        )
+
+    for d in range(1, n):
+        list_copy(peer(d)).start()
+    for c in range(CHUNKS):
+
+        @pl.when(me < n - 1)
+        def _():
+            gather_copy(0, me, c, own=True).start()
+
+        @pl.when(me > 0)
+        def _():
+            gather_copy(1, me, c, own=True).start()
+
+    rows_in[me] = rows_ref[me]
+    cot_all[me] = cot_ref[...]
+
+    scores = scores_ref[...]
+    raised = jnp.exp(scores - jnp.max(scores, axis=1, keepdims=True))
+    share = raised / jnp.sum(raised, axis=1, keepdims=True)
+    weights[...] = share.reshape(picks, tokens)
+
+    place = lax.broadcasted_iota(jnp.int32, (cap, tokens), 0)
+
+    @pl.loop(0, n)
+    def _(owner):
+        first = owner * cap
+        total = jnp.zeros((cap, tokens), F32)
+        for h in range(heads):
+            held = jnp.zeros((cap, tokens), F32)
+            for k in range(topk):
+                p = h * topk + k
+                here = sel_ref[p : p + 1, :] - first
+                held = jnp.where(place == here, weights[p : p + 1, :], held)
+            total = total + held
+        comb_own[owner] = total.astype(BF16)
+
+    for d in range(1, n):
+        comb_copy(peer(d)).start()
+    comb_in[me] = comb_own[me]
+
+    def relay(d):
+        for c in range(CHUNKS):
+
+            @pl.when(me - d >= 0)
+            def _():
+                gather_copy(0, me - d, c).wait_recv()
+
+            @pl.when((me - d >= 0) & (me < n - 1))
+            def _():
+                gather_copy(0, me - d, c).start()
+
+            @pl.when(me + d < n)
+            def _():
+                gather_copy(1, me + d, c).wait_recv()
+
+            @pl.when((me + d < n) & (me > 0))
+            def _():
+                gather_copy(1, me + d, c).start()
+
+    relay(1)
+
+    row_ids = lax.broadcasted_iota(jnp.int32, (table_rows, cap), 0)
+    for d in range(1, n):
+        list_arrival(peer(d)).wait_recv()
+        comb_arrival(peer(d)).wait_recv()
+    for s in range(n):
+        hot[s] = jnp.where(rows_in[s] == row_ids, 1.0, 0.0).astype(BF16)
+        spread[:, s * tokens : (s + 1) * tokens] = jnp.dot(
+            hot[s], comb_in[s], preferred_element_type=F32
+        ).astype(BF16)
+    part[...] = lax.dot_general(
+        spread[...], values_ref[...], (((0,), (0,)), ((), ())), preferred_element_type=F32
+    ).reshape(n, tokens, width)
+
+    def pass_on(t):
+        right_dest = n - 1 - t + me
+        left_dest = t - (n - 1 - me)
+        for c in range(CHUNKS):
+            at = rows_of(c)
+
+            @pl.when((t >= me) & (me == 0))
+            def _():
+                from_left[right_dest, at] = part[right_dest, at].astype(BF16)
+
+            @pl.when((t >= me) & (me > 0))
+            def _():
+                sum_copy(0, right_dest, c).wait_recv()
+                got = from_left[right_dest, at].astype(F32)
+                from_left[right_dest, at] = (got + part[right_dest, at]).astype(BF16)
+
+            @pl.when(t >= me)
+            def _():
+                sum_copy(0, right_dest, c).start()
+
+            @pl.when((left_dest >= 0) & (me == n - 1))
+            def _():
+                from_right[left_dest, at] = part[left_dest, at].astype(BF16)
+
+            @pl.when((left_dest >= 0) & (me < n - 1))
+            def _():
+                sum_copy(1, left_dest, c).wait_recv()
+                got = from_right[left_dest, at].astype(F32)
+                from_right[left_dest, at] = (got + part[left_dest, at]).astype(BF16)
+
+            @pl.when(left_dest >= 0)
+            def _():
+                sum_copy(1, left_dest, c).start()
+
+    def products(source):
+        full = lax.dot_general(
+            cot_all[source],
+            values_ref[...],
+            (((1,), (1,)), ((), ())),
+            preferred_element_type=F32,
+        ).astype(BF16)
+        prod_out[source] = jnp.dot(full, hot[source], preferred_element_type=F32).astype(BF16)
+
+    def products_at(d):
+        @pl.when(me - d >= 0)
+        def _():
+            products(me - d)
+            prod_copy(me - d).start()
+
+        @pl.when(me + d < n)
+        def _():
+            products(me + d)
+            prod_copy(me + d).start()
+
+    pass_on(0)
+    products(me)
+    prod_in[me] = prod_out[me]
+    products_at(1)
+    for d in range(2, n):
+        relay(d)
+        pass_on(d - 1)
+        products_at(d)
+
+    for column in range(0, width, 256):
+        grad_ref[:, column : column + 256] = jnp.dot(
+            spread[...],
+            cot_all[:, :, column : column + 256].reshape(n * tokens, 256),
+            preferred_element_type=F32,
+        ).astype(BF16)
+
+    for d in range(1, n):
+        prod_arrival(peer(d)).wait_recv()
+    chosen = sel_ref[...].T
+    place_of = lax.rem(chosen, cap)
+    owner_of = lax.div(chosen, cap)
+    dots = jnp.zeros((tokens, picks), F32)
+    for o in range(n):
+        found = jnp.take_along_axis(
+            prod_in[o].astype(F32), place_of, axis=1, mode="promise_in_bounds"
+        )
+        dots = jnp.where(owner_of == o, found, dots)
+    dots_in[my_pipe] = dots.T.astype(BF16)
+    for d in range(1, pipes):
+        dots_copy(pipe_peer(d)).start()
+
+    for c in range(CHUNKS):
+        at = rows_of(c)
+        part_here = part[me, at]
+
+        mem_ref[at] = part_here.astype(BF16)
+
+        @pl.when((me > 0) & (me < n - 1))
+        def _():
+            sum_copy(0, me, c).wait_recv()
+            sum_copy(1, me, c).wait_recv()
+            both = from_left[me, at].astype(F32) + from_right[me, at].astype(F32)
+            mem_ref[at] = (part[me, at] + both).astype(BF16)
+
+        @pl.when(me == 0)
+        def _():
+            sum_copy(1, me, c).wait_recv()
+            mem_ref[at] = (part[me, at] + from_right[me, at].astype(F32)).astype(BF16)
+
+        @pl.when(me == n - 1)
+        def _():
+            sum_copy(0, me, c).wait_recv()
+            mem_ref[at] = (part[me, at] + from_left[me, at].astype(F32)).astype(BF16)
+
+    for d in range(1, pipes):
+        dots_arrival(pipe_peer(d)).wait_recv()
+    full_dots = dots_in[0].astype(F32)
+    for q in range(1, pipes):
+        full_dots = full_dots + dots_in[q].astype(F32)
+    full_dots = full_dots.reshape(heads, topk, tokens)
+    w = weights[...].reshape(heads, topk, tokens)
+    dscore_ref[...] = w * (full_dots - jnp.sum(w * full_dots, axis=1, keepdims=True))
+
+    for d in range(1, n):
+        list_copy(peer(d)).wait_send()
+        comb_copy(peer(d)).wait_send()
+        prod_copy(peer(d)).wait_send()
+    for d in range(1, pipes):
+        dots_copy(pipe_peer(d)).wait_send()
+    for c in range(CHUNKS):
+        for d in range(n - 1):
+
+            @pl.when((me - d >= 0) & (me < n - 1))
+            def _():
+                gather_copy(0, me - d, c, own=d == 0).wait_send()
+
+            @pl.when((me + d < n) & (me > 0))
+            def _():
+                gather_copy(1, me + d, c, own=d == 0).wait_send()
+
+        for t in range(n - 1):
+            right_dest = n - 1 - t + me
+            left_dest = t - (n - 1 - me)
+
+            @pl.when(t >= me)
+            def _():
+                sum_copy(0, right_dest, c).wait_send()
+
+            @pl.when(left_dest >= 0)
+            def _():
+                sum_copy(1, left_dest, c).wait_send()
+
+
+def shards_kernel(values, cotangent, scores, row_lists, sel_slot):
+    n, pipes = lax.axis_size("mem"), lax.axis_size("pipe")
+    tokens, width = cotangent.shape
+    heads, topk = scores.shape[1:]
+    table_rows, cap = values.shape[0], row_lists.shape[2]
+    picks = heads * topk
+    dma = pltpu.SemaphoreType.DMA
+    mem_out, grad_values, dscore = pl.pallas_call(
+        functools.partial(kernel, n, pipes, heads, topk),
+        out_shape=(
+            jax.ShapeDtypeStruct((tokens, width), BF16),
+            jax.ShapeDtypeStruct((table_rows, width), BF16),
+            jax.ShapeDtypeStruct((heads, topk, tokens), F32),
+        ),
+        in_specs=[pl.BlockSpec(memory_space=pltpu.VMEM)] * 5,
+        out_specs=[pl.BlockSpec(memory_space=pltpu.VMEM)] * 3,
+        scratch_shapes=[
+            pltpu.VMEM((n, tokens, width), BF16),
+            pltpu.VMEM((picks, tokens), F32),
+            pltpu.VMEM((n, cap, tokens), BF16),
+            pltpu.VMEM((n, cap, tokens), BF16),
+            pltpu.VMEM((n, 1, cap), jnp.int32),
+            pltpu.VMEM((n, table_rows, cap), BF16),
+            pltpu.VMEM((table_rows, n * tokens), BF16),
+            pltpu.VMEM((n, tokens, width), F32),
+            pltpu.VMEM((n, tokens, width), BF16),
+            pltpu.VMEM((n, tokens, width), BF16),
+            pltpu.VMEM((n, tokens, cap), BF16),
+            pltpu.VMEM((n, tokens, cap), BF16),
+            pltpu.VMEM((pipes, picks, tokens), BF16),
+            dma((2, n, CHUNKS)),
+            dma((n, CHUNKS)),
+            dma((n,)),
+            dma((n,)),
+            dma((n,)),
+            dma((n,)),
+            dma((2, n, CHUNKS)),
+            dma((2, n, CHUNKS)),
+            dma((n,)),
+            dma((n,)),
+            dma((pipes,)),
+            dma((pipes,)),
+        ],
+        compiler_params=pltpu.CompilerParams(
+            collective_id=0, has_side_effects=True, vmem_limit_bytes=40 * 1024 * 1024
+        ),
+    )(
+        values,
+        cotangent,
+        scores.transpose(1, 2, 0),
+        row_lists.reshape(n, 1, cap),
+        sel_slot.transpose(1, 2, 0).reshape(picks, tokens),
+    )
+    return mem_out, grad_values, dscore.transpose(2, 0, 1)
+
+
 def solution(mesh):
+    body = shards_kernel if 2 <= mesh.shape["mem"] <= 4 else shards_collective
     placed = (
         P(("dp", "mem"), "pipe"),
         P(("dp", "mem"), "pipe"),
@@ -84,7 +540,7 @@
         P(("dp", "mem"), None, None),
     )
     return jax.shard_map(
-        shards,
+        body,
         mesh=mesh,
         in_specs=placed,
         out_specs=(

time: 103 us -> 50.3 us (0.49)
  waiting for transfers between devices: 44.4 us -> 0 us
  Pallas kernels: 0 us -> 42.5 us
  matrix products: 19.4 us -> 0 us
  blocking collectives: 16.3 us -> 0 us
  starting transfers between devices: 15.1 us -> 0 us
  other arithmetic: 2.89 us -> 0 us
  local copies, waits for them, and re-layouts: 4.05 us -> 6.83 us
    all_to_all x3 -> x0, waiting for transfers between devices: 44.4 us -> none  [the longest x1 22.5 us: shards(): lax.all_to_all(looked, 'mem', split_axis=0, concat_axis=0, tiled=True)]
    pallas_call x0 -> x1, Pallas kernels: none -> 42.5 us  [shards_kernel(): pl.pallas_call(functools.partial(kernel, n, pipes, heads, topk), out_shap...]
    dot_general x7 -> x0, matrix products: 19.4 us -> none  [the longest x1 8.1 us: shards(): jnp.einsum('tpc,toc->tpo', place_hot, products, precision=highest, prefer...]
    psum x1 -> x0, blocking collectives: 16.3 us -> none  [shards(): lax.psum(partial_dots.astype(jnp.bfloat16), 'pipe').astype(jnp.float32)]
    all_to_all x3 -> x0, starting transfers between devices: 15.1 us -> none  [the longest x1 6.46 us: shards(): lax.all_to_all(row_lists[0], 'mem', split_axis=0, concat_axis=0, tiled=True)]
    unnamed x18 -> x13, local copies, waits for them, and re-layouts: 0.59 us -> 6.83 us
    gather x1 -> x0, local copies, waits for them, and re-layouts: 2.06 us -> none  [shards(): looked = jnp.take(values, jnp.maximum(asked, 0), axis=0)]
    select_n x2 -> x0, other arithmetic: 1.26 us -> none  [the longest x1 1.2 us: shards(): looked = jnp.where(present[..., None], looked, jnp.zeros_like(looked))]
  transfers between devices with their start and end apart: 3 -> 0, of which waited for: 2 -> 0; matrix products, arithmetic and copies ran while one was open for 15% -> 0% of each run, Pallas kernels for 0% -> 0%
where the time goes in v1:
time: 50.3 us; the launch traced here: 50 us
  Pallas kernels  42.5 us (84%)
  local copies, waits for them, and re-layouts  6.83 us (14%)
  between operations  0.65 us (1%)
    pallas_call x1, Pallas kernels, shards_kernel(): pl.pallas_call(functools.partial(kernel, n, pipes, heads, topk), out_shap...  42.5 us
    unnamed x13, local copies, waits for them, and re-layouts  6.83 us

profile of v1, /device:TPU:0, one launch (start us, length us, event | category | flops | bytes accessed | tf_op | source)
XLA Modules:
  0.0 50.0 jit_solution(8674943388764257904)
XLA Ops:
  0.6 0.0 copy-start.4
  0.6 0.7 %copy-done.4 = s32[1,4,128]{2,1,0:T(4,128)S(1)} copy-done((s32[1,4,128]{2,1,0:T(4,128)S(1)}, s32[1,4,128]{2,1,0:T(4,128)}, u32[]{:S(2)}) %copy-start.4) | copy-done | bytes 2072
  1.3 0.0 copy-start
  1.3 1.2 %copy-done = bf16[512,1024]{1,0:T(8,128)(2,1)S(1)} copy-done((bf16[512,1024]{1,0:T(8,128)(2,1)S(1)}, bf16[512,1024]{1,0:T(8,128)(2,1)}, u32[]{:S(2)}) %copy-start) | copy-done | bytes 1048600
  2.5 0.0 copy-start.1
  2.5 0.9 %copy-done.1 = bf16[128,1024]{1,0:T(8,128)(2,1)S(1)} copy-done((bf16[128,1024]{1,0:T(8,128)(2,1)S(1)}, bf16[128,1024]{1,0:T(8,128)(2,1)}, u32[]{:S(2)}) %copy-start.1) | copy-done | bytes 262168
  3.5 0.0 copy-start.2
  3.5 0.8 %copy-done.2 = f32[128,4,32]{0,2,1:T(8,128)S(1)} copy-done((f32[128,4,32]{0,2,1:T(8,128)S(1)}, f32[128,4,32]{0,2,1:T(8,128)}, u32[]{:S(2)}) %copy-start.2) | copy-done | bytes 65560
  4.3 0.0 copy-start.3
  4.3 0.8 %copy-done.3 = s32[128,4,32]{0,2,1:T(8,128)S(1)} copy-done((s32[128,4,32]{0,2,1:T(8,128)S(1)}, s32[128,4,32]{0,2,1:T(8,128)}, u32[]{:S(2)}) %copy-start.3) | copy-done | bytes 65560
  5.2 42.5 %shard_map.76 = (bf16[128,1024]{1,0:T(8,128)(2,1)S(1)}, bf16[512,1024]{1,0:T(8,128)(2,1)S(1)}, f32[4,32,128]{2,1,0:T(8,128)S(1)}) custom-call(bf16[512,1024]{1,0:T(8,128)(2,1)S(1)} %copy-done, bf16[128,1024]{1,0:T(8,128)(2,1)S(1)} %copy-done.1, f32[4,32,128]{2,1,0:T(8,128)S(1)} %bitcast.6, s32[4,1,128]{2,1,0:T(1,128)S(1)} %bitcast.9, s32[128,128]{1,0:T(8,128)S(1)} %bitcast.7), custom_call_target="tpu_custom_call" | custom-call | tf_op jit(solution)/shard_map/pallas_call | solution.py:484
  47.7 0.7 %copy.11 = bf16[128,1024]{1,0:T(8,128)(2,1)} copy(bf16[128,1024]{1,0:T(8,128)(2,1)S(1)} %get-tuple-element.12) | data formatting | bytes 524288
  48.4 1.0 %copy.12 = bf16[512,1024]{1,0:T(8,128)(2,1)} copy(bf16[512,1024]{1,0:T(8,128)(2,1)S(1)} %get-tuple-element.13) | data formatting | bytes 2097152
  49.4 0.6 %copy.13 = f32[128,4,32]{0,2,1:T(8,128)} copy(f32[128,4,32]{0,2,1:T(8,128)S(1)} %bitcast.8) | data formatting | bytes 131072
Async XLA Ops:
  0.6 0.7 %copy-start.4 = (s32[1,4,128]{2,1,0:T(4,128)S(1)}, s32[1,4,128]{2,1,0:T(4,128)}, u32[]{:S(2)}) copy-start(s32[1,4,128]{2,1,0:T(4,128)} %param.8) | copy-start | bytes 6148
  1.3 1.2 %copy-start = (bf16[512,1024]{1,0:T(8,128)(2,1)S(1)}, bf16[512,1024]{1,0:T(8,128)(2,1)}, u32[]{:S(2)}) copy-start(bf16[512,1024]{1,0:T(8,128)(2,1)} %values_ref.1) | copy-start | bytes 3145732
  2.5 0.9 %copy-start.1 = (bf16[128,1024]{1,0:T(8,128)(2,1)S(1)}, bf16[128,1024]{1,0:T(8,128)(2,1)}, u32[]{:S(2)}) copy-start(bf16[128,1024]{1,0:T(8,128)(2,1)} %cot_ref.1) | copy-start | bytes 786436
  3.5 0.8 %copy-start.2 = (f32[128,4,32]{0,2,1:T(8,128)S(1)}, f32[128,4,32]{0,2,1:T(8,128)}, u32[]{:S(2)}) copy-start(f32[128,4,32]{0,2,1:T(8,128)} %param.7) | copy-start | bytes 196612
  4.3 0.8 %copy-start.3 = (s32[128,4,32]{0,2,1:T(8,128)S(1)}, s32[128,4,32]{0,2,1:T(8,128)}, u32[]{:S(2)}) copy-start(s32[128,4,32]{0,2,1:T(8,128)} %param.9) | copy-start | bytes 196612

commit v2 on v1

--- a/solution.py
+++ b/solution.py
@@ -80,7 +80,7 @@
 
 
 MESH = pl.DeviceIdType.MESH
-CHUNKS = 4
+CHUNKS = 2
 F32 = jnp.float32
 BF16 = jnp.bfloat16
 
@@ -90,14 +90,17 @@
     pipes,
     heads,
     topk,
-    values_ref,
+    values_hbm,
     cot_ref,
-    scores_ref,
+    scores_hbm,
     rows_ref,
-    sel_ref,
+    sel_hbm,
     mem_ref,
     grad_ref,
     dscore_ref,
+    values_ref,
+    scores_ref,
+    sel_ref,
     cot_all,
     weights,
     comb_own,
@@ -123,11 +126,12 @@
     pr_recv,
     dt_send,
     dt_recv,
+    local_sem,
 ):
     me = lax.axis_index("mem")
     my_pipe = lax.axis_index("pipe")
     tokens, width = cot_ref.shape
-    table_rows = values_ref.shape[0]
+    table_rows = values_hbm.shape[0]
     cap = rows_ref.shape[2]
     step = tokens // CHUNKS
     picks = heads * topk
@@ -137,6 +141,21 @@
 
     def pipe_peer(d):
         return lax.rem(my_pipe + d, pipes)
+
+    local = [
+        pltpu.make_async_copy(src, dst, local_sem.at[i])
+        for i, (src, dst) in enumerate(
+            (
+                (scores_hbm, scores_ref),
+                (sel_hbm, sel_ref),
+                (rows_ref.at[me], rows_in.at[me]),
+                (cot_ref, cot_all.at[me]),
+                (values_hbm, values_ref),
+            )
+        )
+    ]
+    for copy in local:
+        copy.start()
 
     barrier = pltpu.get_barrier_semaphore()
     for d in range(1, n):
@@ -266,9 +285,8 @@
         def _():
             gather_copy(1, me, c, own=True).start()
 
-    rows_in[me] = rows_ref[me]
-    cot_all[me] = cot_ref[...]
-
+    local[0].wait()
+    local[1].wait()
     scores = scores_ref[...]
     raised = jnp.exp(scores - jnp.max(scores, axis=1, keepdims=True))
     share = raised / jnp.sum(raised, axis=1, keepdims=True)
@@ -313,6 +331,8 @@
                 gather_copy(1, me + d, c).start()
 
     relay(1)
+    for copy in local[2:]:
+        copy.wait()
 
     row_ids = lax.broadcasted_iota(jnp.int32, (table_rows, cap), 0)
     for d in range(1, n):
@@ -327,38 +347,39 @@
         spread[...], values_ref[...], (((0,), (0,)), ((), ())), preferred_element_type=F32
     ).reshape(n, tokens, width)
 
+    def open_line():
+        for i in range(n - 1):
+
+            @pl.when(me == 0)
+            def _():
+                from_left[n - 1 - i] = part[n - 1 - i].astype(BF16)
+                for c in range(CHUNKS):
+                    sum_copy(0, n - 1 - i, c).start()
+
+            @pl.when(me == n - 1)
+            def _():
+                from_right[i] = part[i].astype(BF16)
+                for c in range(CHUNKS):
+                    sum_copy(1, i, c).start()
+
     def pass_on(t):
         right_dest = n - 1 - t + me
         left_dest = t - (n - 1 - me)
         for c in range(CHUNKS):
             at = rows_of(c)
 
-            @pl.when((t >= me) & (me == 0))
-            def _():
-                from_left[right_dest, at] = part[right_dest, at].astype(BF16)
-
             @pl.when((t >= me) & (me > 0))
             def _():
                 sum_copy(0, right_dest, c).wait_recv()
                 got = from_left[right_dest, at].astype(F32)
                 from_left[right_dest, at] = (got + part[right_dest, at]).astype(BF16)
-
-            @pl.when(t >= me)
-            def _():
                 sum_copy(0, right_dest, c).start()
-
-            @pl.when((left_dest >= 0) & (me == n - 1))
-            def _():
-                from_right[left_dest, at] = part[left_dest, at].astype(BF16)
 
             @pl.when((left_dest >= 0) & (me < n - 1))
             def _():
                 sum_copy(1, left_dest, c).wait_recv()
                 got = from_right[left_dest, at].astype(F32)
                 from_right[left_dest, at] = (got + part[left_dest, at]).astype(BF16)
-
-            @pl.when(left_dest >= 0)
-            def _():
                 sum_copy(1, left_dest, c).start()
 
     def products(source):
@@ -381,7 +402,7 @@
             products(me + d)
             prod_copy(me + d).start()
 
-    pass_on(0)
+    open_line()
     products(me)
     prod_in[me] = prod_out[me]
     products_at(1)
@@ -414,9 +435,6 @@
 
     for c in range(CHUNKS):
         at = rows_of(c)
-        part_here = part[me, at]
-
-        mem_ref[at] = part_here.astype(BF16)
 
         @pl.when((me > 0) & (me < n - 1))
         def _():
@@ -474,6 +492,15 @@
                 sum_copy(1, left_dest, c).wait_send()
 
 
+def finish(mem_ref, grad_ref, dscore_ref, mem_out, grad_out, dscore_out, sems):
+    pairs = ((grad_ref, grad_out), (mem_ref, mem_out), (dscore_ref, dscore_out))
+    copies = [pltpu.make_async_copy(a, b, sems.at[i]) for i, (a, b) in enumerate(pairs)]
+    for copy in copies:
+        copy.start()
+    for copy in copies:
+        copy.wait()
+
+
 def shards_kernel(values, cotangent, scores, row_lists, sel_slot):
     n, pipes = lax.axis_size("mem"), lax.axis_size("pipe")
     tokens, width = cotangent.shape
@@ -481,16 +508,20 @@
     table_rows, cap = values.shape[0], row_lists.shape[2]
     picks = heads * topk
     dma = pltpu.SemaphoreType.DMA
-    mem_out, grad_values, dscore = pl.pallas_call(
+    shapes = (
+        jax.ShapeDtypeStruct((tokens, width), BF16),
+        jax.ShapeDtypeStruct((table_rows, width), BF16),
+        jax.ShapeDtypeStruct((heads, topk, tokens), F32),
+    )
+    results = pl.pallas_call(
         functools.partial(kernel, n, pipes, heads, topk),
-        out_shape=(
-            jax.ShapeDtypeStruct((tokens, width), BF16),
-            jax.ShapeDtypeStruct((table_rows, width), BF16),
-            jax.ShapeDtypeStruct((heads, topk, tokens), F32),
-        ),
-        in_specs=[pl.BlockSpec(memory_space=pltpu.VMEM)] * 5,
+        out_shape=shapes,
+        in_specs=[pl.BlockSpec(memory_space=pl.ANY)] * 5,
         out_specs=[pl.BlockSpec(memory_space=pltpu.VMEM)] * 3,
         scratch_shapes=[
+            pltpu.VMEM((table_rows, width), BF16),
+            pltpu.VMEM((heads, topk, tokens), F32),
+            pltpu.VMEM((picks, tokens), jnp.int32),
             pltpu.VMEM((n, tokens, width), BF16),
             pltpu.VMEM((picks, tokens), F32),
             pltpu.VMEM((n, cap, tokens), BF16),
@@ -516,9 +547,10 @@
             dma((n,)),
             dma((pipes,)),
             dma((pipes,)),
+            dma((5,)),
         ],
         compiler_params=pltpu.CompilerParams(
-            collective_id=0, has_side_effects=True, vmem_limit_bytes=40 * 1024 * 1024
+            collective_id=0, has_side_effects=True, vmem_limit_bytes=63 * 1024 * 1024
         ),
     )(
         values,
@@ -527,6 +559,13 @@
         row_lists.reshape(n, 1, cap),
         sel_slot.transpose(1, 2, 0).reshape(picks, tokens),
     )
+    mem_out, grad_values, dscore = pl.pallas_call(
+        finish,
+        out_shape=shapes,
+        in_specs=[pl.BlockSpec(memory_space=pltpu.VMEM)] * 3,
+        out_specs=[pl.BlockSpec(memory_space=pl.ANY)] * 3,
+        scratch_shapes=[dma((3,))],
+    )(*results)
     return mem_out, grad_values, dscore.transpose(2, 0, 1)
 
 

time: 50.3 us -> 46.5 us (0.924)
  local copies, waits for them, and re-layouts: 6.83 us -> 0 us
  Pallas kernels: 42.5 us -> 45.7 us
    unnamed x13 -> x0, local copies, waits for them, and re-layouts: 6.83 us -> none
    pallas_call x0 -> x1, Pallas kernels: none -> 2.35 us  [shards_kernel(): pl.pallas_call(finish, out_shape=shapes, in_specs=[pl.BlockSpec(memory_sp...]
    pallas_call x1, Pallas kernels: 42.5 us -> 43.4 us  [shards_kernel(): pl.pallas_call(functools.partial(kernel, n, pipes, heads, topk), out_shap...]
where the time goes in v2:
time: 46.5 us; the launch traced here: 46.4 us
  Pallas kernels  45.7 us (98%)
  between operations  0.64 us (1%)
    pallas_call x1, Pallas kernels, shards_kernel(): pl.pallas_call(functools.partial(kernel, n, pipes, heads, topk), out_shap...  43.4 us
    pallas_call x1, Pallas kernels, shards_kernel(): pl.pallas_call(finish, out_shape=shapes, in_specs=[pl.BlockSpec(memory_sp...  2.35 us

profile of v2, /device:TPU:0, one launch (start us, length us, event | category | flops | bytes accessed | tf_op | source)
XLA Modules:
  0.0 46.4 jit_solution(4420967112326265190)
XLA Ops:
  0.6 43.4 %shard_map.76 = (bf16[128,1024]{1,0:T(8,128)(2,1)}, bf16[512,1024]{1,0:T(8,128)(2,1)}, f32[4,32,128]{2,1,0:T(8,128)}) custom-call(bf16[512,1024]{1,0:T(8,128)(2,1)} %values_hbm.1, bf16[128,1024]{1,0:T(8,128)(2,1)} %cot_ref.1, f32[4,32,128]{2,1,0:T(8,128)} %bitcast.6, s32[4,1,128]{2,1,0:T(1,128)} %bitcast.8, s32[128,128]{1,0:T(8,128)} %bitcast.7), custom_call_target="tpu_custom_call" | custom-call | tf_op jit(solution)/shard_map/pallas_call | solution.py:516
  44.0 2.4 %shard_map.77 = (bf16[128,1024]{1,0:T(8,128)(2,1)}, bf16[512,1024]{1,0:T(8,128)(2,1)}, f32[4,32,128]{2,1,0:T(8,128)}) custom-call(bf16[128,1024]{1,0:T(8,128)(2,1)} %get-tuple-element.9.mem_ref, bf16[512,1024]{1,0:T(8,128)(2,1)} %get-tuple-element.10.grad_ref, f32[4,32,128]{2,1,0:T(8,128)} %get-tuple-element.11.dscore_ref), custom_call_target="tpu_custom_call" | custom-call | tf_op jit(solution)/shard_map/pallas_call | solution.py:562
